TPU v7x, 32 devices: a whole 2x2x4 slice. The times are simulated.
32 devices in a mesh: wave: 8 (over z, y), lon: 4 (over x, core).
Axes of the slice: x: 2, y: 2, z: 4, core: 2. Of those that a mesh axis runs over, the one named last changes fastest.
Arguments:
- spectra: bfloat16 [640, 2, 3, 8, 1281], P('wave', None, None, 'lon'), may hold values from -6 to 6
- legendre: bfloat16 [640, 8, 1281], P('wave'), may hold values from -0.0034179688 to 0.0034179688
- pair_waves: int32 [640], replicated, may hold values from 0 to 639, each once
- row_lengths: int32 [8], P('wave'), may hold values from 1280 to 5120, as said below
- departure: int32 [8, 8, 4, 1280], P('wave', None, 'lon'), may hold values from -7 to 6
- weights: bfloat16 [4, 8, 8, 4, 1280], P(None, 'wave', None, 'lon'), may hold values from -0.29882812 to 0.796875
Outputs:
- departed: bfloat16 [3, 8, 8, 4, 1280], P(None, 'wave', None, 'lon')
Inputs may be any that keep to these rules, and one draw needn't show every extreme that they name: Pair slot p holds wavenumbers pair_waves[p] and 1279 - pair_waves[p]; every value appears once. `row_lengths`: every row length is a multiple of 8.
All inputs are finite; a program needn't handle non-finite values.
Results may differ from a plain program's by a relative error of at most 0.0059.
Values may be sent and summed in bfloat16 or wider, within the bound.
A program may use at most 192 MiB of HBM per device.

v0:
```python
import math

import jax
import jax.numpy as jnp
from jax import lax
from jax.sharding import PartitionSpec as P

TRUNC = 1279
HALO = 8


def passed_along(block, axis, distance):
    devices = range(lax.axis_size(axis))
    route = [((i - distance) % len(devices), i) for i in devices]
    return lax.ppermute(block, axis, route)


def build_tables(wavenumbers, lengths, segment, seg_width, seg_count):
    seg_share = lengths // seg_count
    slot_index = jnp.arange(seg_width, dtype=jnp.int32)
    longitude = segment * seg_share[:, None] + slot_index[None, :]
    inside = (slot_index[None, :] < seg_share[:, None]).astype(jnp.float32)
    row_len = lengths[:, None, None, None]
    wave_grid = wavenumbers[None, :, :, None]
    residue = wave_grid * longitude[:, None, None, :] % row_len
    angles = 2.0 * math.pi * residue.astype(jnp.float32) / row_len.astype(jnp.float32)
    highest = row_len // 2 - 1
    factor = jnp.where(wave_grid == 0, 1.0, jnp.where(wave_grid <= highest, 2.0, 0.0)).astype(
        jnp.float32
    )
    factor = factor * inside[:, None, None, :]
    cosine = (factor * jnp.cos(angles)).astype(jnp.bfloat16)
    sines = (-factor * jnp.sin(angles)).astype(jnp.bfloat16)
    return (cosine, sines)


def synthesize_with(coeffs, cosine, sines):
    real_part = jnp.einsum(
        "pwfvj,jpwk->jfvk", coeffs[:, :, 0], cosine, preferred_element_type=jnp.float32
    )
    imag_part = jnp.einsum(
        "pwfvj,jpwk->jfvk", coeffs[:, :, 1], sines, preferred_element_type=jnp.float32
    )
    return (real_part + imag_part).astype(jnp.bfloat16)


def local(spectra, legendre, pair_waves, row_lengths, departure, weights):
    pair_dev = spectra.shape[0]
    level_dev = spectra.shape[3]
    packed = spectra.shape[4]
    row_total = legendre.shape[1]
    columns = 6 * level_dev
    start_pair = lax.axis_index("wave") * pair_dev
    own_waves = lax.dynamic_slice_in_dim(pair_waves, start_pair, pair_dev)
    flat_spec = spectra.reshape(pair_dev, columns, packed)
    keeper = jnp.arange(packed, dtype=jnp.int32)[None, :] < (TRUNC + 1 - own_waves)[:, None]
    keeper = keeper[:, None, :]
    blank = jnp.zeros_like(flat_spec)
    doubled = jnp.stack(
        [jnp.where(keeper, flat_spec, blank), jnp.where(keeper, blank, flat_spec)], axis=1
    )
    fourier = jnp.einsum("pwcn,pln->pwcl", doubled, legendre, preferred_element_type=jnp.float32)
    fourier = fourier.astype(jnp.bfloat16).reshape(pair_dev, 2, 2, 3, level_dev, row_total)
    by_rows = lax.all_to_all(fourier, "wave", split_axis=5, concat_axis=0, tiled=True)
    wavenumbers = jnp.stack([pair_waves, TRUNC - pair_waves], axis=1)
    seg_width = departure.shape[3]
    seg_count = lax.axis_size("lon")
    cosine, sines = build_tables(
        wavenumbers, row_lengths, lax.axis_index("lon"), seg_width, seg_count
    )
    grid = synthesize_with(lax.all_gather(by_rows, "lon", axis=4, tiled=True), cosine, sines)
    seg_share = row_lengths // seg_count
    rim_index = seg_share[:, None] - HALO + jnp.arange(HALO, dtype=jnp.int32)[None, :]
    rim_shape = grid.shape[:3] + (HALO,)
    tail_cells = jnp.take_along_axis(
        grid, jnp.broadcast_to(rim_index[:, None, None, :], rim_shape), axis=3
    )
    head_cells = grid[:, :, :, :HALO]
    west = passed_along(tail_cells, "lon", 1)
    east = passed_along(head_cells, "lon", -1)
    extended = jnp.concatenate([west, grid, east], axis=3)
    ext_len = extended.shape[3]
    offsets = departure[:, :, 0, :]
    slot_index = jnp.arange(seg_width, dtype=jnp.int32)
    share_wide = seg_share[:, None, None]
    total = jnp.zeros(grid.shape, jnp.float32)
    for corner in range(4):
        target = slot_index[None, None, :] + offsets + (corner - 1)
        position = jnp.where(
            target < 0,
            target + HALO,
            jnp.where(target >= share_wide, target - share_wide + seg_width + HALO, target + HALO),
        )
        position = jnp.clip(position, 0, ext_len - 1)
        picked = jnp.take_along_axis(
            extended, jnp.broadcast_to(position[:, None, :, :], grid.shape), axis=3
        )
        factor = weights[corner, :, :, 0, :][:, None, :, :].astype(jnp.float32)
        total = total + factor * picked.astype(jnp.float32)
    inside = slot_index[None, :] < seg_share[:, None]
    total = jnp.where(inside[:, None, None, :], total, jnp.zeros_like(total))
    result = jnp.moveaxis(total.astype(jnp.bfloat16), 1, 0)
    return result[:, :, :, None, :]


def solution(mesh):
    return jax.shard_map(
        local,
        mesh=mesh,
        in_specs=(
            P("wave", None, None, "lon", None),
            P("wave", None, None),
            P(),
            P("wave"),
            P("wave", None, "lon", None),
            P(None, "wave", None, "lon", None),
        ),
        out_specs=P(None, "wave", None, "lon", None),
        check_vma=False,
    )
```

profile of v0, /device:TPU:0, one launch (start us, length us, event | category | flops | bytes accessed | tf_op | source)
XLA Modules:
  0.0 1388.6 jit_solution(7328203643109906777)
XLA Ops:
  0.0 0.9 dynamic-slice_subtract_fusion
  0.9 0.1 iota_compare_fusion
  1.0 2.1 copy.20
  3.1 1.8 copy_select_fusion.1
  4.9 9.4 fusion.35
  14.3 0.4 copy.23
  14.7 0.7 copy.24
  15.3 7.3 all-to-all-start
  23.9 5.5 all-to-all-done
  29.4 0.1 reshape.516
  29.6 5.4 all_gather.3
  35.0 0.2 fusion.77
  35.1 86.3 %fusion.28 = f32[3,8,1280]{2,1,0:T(8,128)S(1)} fusion(f32[1280]{0:T(1024)S(1)} %fusion.67, f32[640,2]{0,1:T(2,128)S(1)} %compare_select_fusion.1, f32[]{:T(128)} %bitcast.17, pred[]{:T(512)} %bitcast.16, s32[]{:T(128)} %bitcast.15, s32[1280]{0:T(1024)S(1)} %iota_add_fusion, s32[640,2]{0,1:T(2,128)S(1)} %pad_add_fusion, ...), kind=kOutput, calls=%fused_computation.31 | convolution fusion | flops 101580800 | bytes 204809 | tf_op jit(solution)/shard_map/pwfvj,jpwk->jfvk/dot_general | solution.py:38
  121.5 98.9 %fusion.31 = bf16[3,8,1280]{2,1,0:T(8,128)(2,1)S(1)} fusion(f32[3,8,1280]{2,1,0:T(8,128)S(1)} %fusion.28, f32[1280]{0:T(1024)S(1)} %fusion.67, f32[640,2]{0,1:T(2,128)S(1)} %compare_select_fusion.1, f32[]{:T(128)} %bitcast.17, pred[]{:T(512)} %bitcast.16, s32[]{:T(128)} %bitcast.15, s32[1280]{0:T(1024)S(1)} %iota_add_fusion, s32[640,2]{0,1:T(2,128)S(1)} %pad_add_fusion, ...), kind=kOutput, calls=%fused_computation.32 | convolution fusion | flops 103280640 | bytes 266249 | tf_op jit(solution)/shard_map/pwfvj,jpwk->jfvk/dot_general | solution.py:41
  220.4 2.2 gather_fusion
  222.7 0.4 collective-permute-start
  223.1 1.4 collective-permute-start.1
  224.6 1.3 collective-permute-done
  225.9 0.1 concatenate.10
  226.0 290.3 %gather_fusion.1 = bf16[30720]{0:T(1024)(128)(2,1)S(1)} fusion(bf16[3,8,1296]{2,1,0:T(8,128)(2,1)S(1)} %bitcast.132, s32[30720]{0:T(1024)S(1)} %reshape.489), kind=kCustom, calls=%fused_computation.clone | custom fusion | bytes 491520 | tf_op jit(solution)/shard_map/jit(take_along_axis)/gather | solution.py:95
  516.4 290.3 %gather_fusion.2 = bf16[30720]{0:T(1024)(128)(2,1)S(1)} fusion(bf16[3,8,1296]{2,1,0:T(8,128)(2,1)S(1)} %bitcast.133, s32[30720]{0:T(1024)S(1)} %reshape.495), kind=kCustom, calls=%fused_computation.1.clone | custom fusion | bytes 491520 | tf_op jit(solution)/shard_map/jit(take_along_axis)/gather | solution.py:95
  806.8 290.3 %gather_fusion.3 = bf16[30720]{0:T(1024)(128)(2,1)S(1)} fusion(bf16[3,8,1296]{2,1,0:T(8,128)(2,1)S(1)} %bitcast.134, s32[30720]{0:T(1024)S(1)} %reshape.501), kind=kCustom, calls=%fused_computation.2.clone | custom fusion | bytes 491520 | tf_op jit(solution)/shard_map/jit(take_along_axis)/gather | solution.py:95
  1097.2 290.3 %gather_fusion.4 = bf16[30720]{0:T(1024)(128)(2,1)S(1)} fusion(bf16[3,8,1296]{2,1,0:T(8,128)(2,1)S(1)} %bitcast.135, s32[30720]{0:T(1024)S(1)} %reshape.507), kind=kCustom, calls=%fused_computation.3.clone | custom fusion | bytes 491520 | tf_op jit(solution)/shard_map/jit(take_along_axis)/gather | solution.py:95
  1387.7 0.8 fusion.60
  (41 shorter events, 1.0 us)
Async XLA Ops:
  0.0 4.9 copy-start
  4.9 18.4 %copy-start.3 = (s32[640]{0:T(1024)S(1)}, s32[640]{0:T(1024)}, u32[]{:S(2)}) copy-start(s32[640]{0:T(1024)} %param.10) | copy-start | bytes 7684
  4.9 18.6 %copy-start.2 = (s32[1,8,1,1280]{3,2,1,0:T(1,128)S(1)}, s32[1,8,1,1280]{3,2,1,0:T(1,128)}, u32[]{:S(2)}) copy-start(s32[1,8,1,1280]{3,2,1,0:T(1,128)} %param.12) | copy-start | bytes 122884
  4.9 18.7 %copy-start.1 = (bf16[4,1,8,1,1280]{4,2,3,1,0:T(8,128)(2,1)S(1)}, bf16[4,1,8,1,1280]{4,2,3,1,0:T(8,128)(2,1)}, u32[]{:S(2)}) copy-start(bf16[4,1,8,1,1280]{4,2,3,1,0:T(8,128)(2,1)} %param.13) | copy-start | bytes 245764
  15.3 14.1 %all-to-all-start = ((bf16[80,2,2,3,2,8]{0,4,3,2,1,5:T(2,128)(2,1)}), bf16[80,2,2,3,2,8]{0,4,3,2,1,5:T(2,128)(2,1)S(1)}, u32[]{:S(2)}, u32[]{:S(2)}) async-start(bf16[80,2,2,3,2,8]{0,4,3,2,1,5:T(2,128)(2,1)} %copy.24), calls=%async_computation | async-start | bytes 98304 | tf_op jit(solution)/shard_map/all_to_all | solution.py:64
  222.7 3.1 collective-permute-start
  223.1 2.8 collective-permute-start.1
where the time goes:
time: 1390 us
  local copies, waits for them, and re-layouts  1170 us (84%)
  matrix products  195 us (14%)
    gather x12, local copies, waits for them, and re-layouts, local(): jnp.take_along_axis(extended, jnp.broadcast_to(position[:, None, :, :], g...  1160 us
    dot_general x1, matrix products, synthesize_with(): jnp.einsum('pwfvj,jpwk->jfvk', coeffs[:, :, 1], sines, preferred_element_...  98.9 us
    dot_general x1, matrix products, synthesize_with(): jnp.einsum('pwfvj,jpwk->jfvk', coeffs[:, :, 0], cosine, preferred_element...  86.3 us
  transfers between devices with their start and end apart: 3, of which 2 were waited for; matrix products, arithmetic and copies ran while one was open for 0% of the time, Pallas kernels for 0%

commit v1 on v0

v1 whole, which is shorter than its diff:
```python
import functools
import math

import jax
import jax.numpy as jnp
from jax import lax
from jax.experimental import pallas as pl
from jax.experimental.pallas import tpu as pltpu
from jax.sharding import PartitionSpec as P

TRUNC = 1279
HALO = 8
LANES = 128
SHIFTS = 2 * HALO + 1
SPAN = LANES + 2 * HALO


def unit_circle(waves, points, length, inverse):
    product = waves * points
    turns = jnp.floor(product * inverse + 0.5)
    half = (product - turns * length) * (inverse * math.pi)
    sq = half * half
    sine, cosine = 0.0, 0.0
    for k in range(7, -1, -1):
        sine = sine * sq + (-1.0) ** k / math.factorial(2 * k + 1)
        cosine = cosine * sq + (-1.0) ** k / math.factorial(2 * k)
    sine = sine * half
    return 1.0 - 2.0 * sine * sine, 2.0 * sine * cosine


def make_tables(seg_count, pairs_ref, length, table_ref, start_cos, start_sin):
    first = pairs_ref[...].astype(jnp.float32)
    waves = jnp.concatenate([first, TRUNC - first], axis=1)
    modes = waves.shape[1]
    length_f = length.astype(jnp.float32)
    inverse = 1.0 / jnp.full((1, 1), length_f, jnp.float32)
    fine_at = lax.broadcasted_iota(jnp.int32, (16, modes), 0).astype(jnp.float32)
    cos_f, sin_f = unit_circle(waves, fine_at, length_f, inverse)
    cos_c, sin_c = unit_circle(waves, fine_at * 16.0, length_f, inverse)
    for a in range(SPAN // 16):
        ca, sa = cos_c[a : a + 1], sin_c[a : a + 1]
        rows = slice(16 * a, 16 * a + 16)
        table_ref[rows, :modes] = (cos_f * ca - sin_f * sa).astype(jnp.bfloat16)
        table_ref[rows, modes:] = (-(sin_f * ca + cos_f * sa)).astype(jnp.bfloat16)
    share = length // seg_count
    start = (lax.axis_index("lon") * share - HALO).astype(jnp.float32)
    cos_s, sin_s = unit_circle(waves, fine_at * float(LANES) + start, length_f, inverse)
    highest = (length // 2 - 1).astype(jnp.float32)
    factor = jnp.where(waves == 0.0, 1.0, jnp.where(waves <= highest, 2.0, 0.0))
    start_cos[...] = cos_s * factor
    start_sin[...] = sin_s * factor


def synthesize(real, imag, blocks, table_ref, start_cos, start_sin, lhs_ref, grid_ref):
    rows, modes = real.shape
    for h in range(blocks):
        c, s = start_cos[h : h + 1], start_sin[h : h + 1]
        at = slice(h * rows, (h + 1) * rows)
        lhs_ref[at, :modes] = real * c - imag * s
        lhs_ref[at, modes:] = real * s + imag * c
    grid_ref[:, :SPAN] = lax.dot_general(
        lhs_ref[...].astype(jnp.bfloat16),
        table_ref[...],
        (((1,), (1,)), ((), ())),
        preferred_element_type=jnp.float32,
    )


def depart(share, blocks, levels, departure_ref, weights_ref, grid_ref, out_ref):
    rows = 3 * levels
    for h in range(blocks):
        lanes = slice(h * LANES, (h + 1) * LANES)
        cell = departure_ref[:, lanes]
        factors = [weights_ref[c, :, lanes].astype(jnp.float32) for c in range(4)]
        totals = [jnp.zeros((levels, LANES), jnp.float32)] * 3
        for s in range(SHIFTS):
            weight = jnp.zeros((levels, LANES), jnp.float32)
            for c in range(4):
                if 1 - HALO <= s - 7 - c <= HALO - 2:
                    weight = weight + jnp.where(cell == s - 7 - c, factors[c], 0.0)
            moved = grid_ref[h * rows : (h + 1) * rows, s : s + LANES]
            for f in range(3):
                totals[f] = totals[f] + weight * moved[f * levels : (f + 1) * levels]
        slot = h * LANES + lax.broadcasted_iota(jnp.int32, (levels, LANES), 1)
        for f in range(3):
            kept = jnp.where(slot < share, totals[f], 0.0)
            out_ref[f, :, lanes] = kept.astype(jnp.bfloat16)


def row_kernel(
    seg_count, length_ref, pairs_ref, fourier_ref, departure_ref, weights_ref, out_ref,
    table_ref, start_cos, start_sin, lhs_ref, grid_ref,
):
    length = length_ref[0]
    levels, width = departure_ref.shape
    blocks = width // LANES
    make_tables(seg_count, pairs_ref, length, table_ref, start_cos, start_sin)
    real = fourier_ref[0].astype(jnp.float32)
    imag = fourier_ref[1].astype(jnp.float32)
    synthesize(real, imag, blocks, table_ref, start_cos, start_sin, lhs_ref, grid_ref)
    depart(length // seg_count, blocks, levels, departure_ref, weights_ref, grid_ref, out_ref)


def local(spectra, legendre, pair_waves, row_lengths, departure, weights):
    pair_dev = spectra.shape[0]
    level_dev = spectra.shape[3]
    packed = spectra.shape[4]
    row_total = legendre.shape[1]
    pairs = pair_waves.shape[0]
    levels, width = departure.shape[1], departure.shape[3]
    seg_count = lax.axis_size("lon")
    columns = 6 * level_dev
    start_pair = lax.axis_index("wave") * pair_dev
    own_waves = lax.dynamic_slice_in_dim(pair_waves, start_pair, pair_dev)
    flat_spec = spectra.reshape(pair_dev, columns, packed)
    keeper = jnp.arange(packed, dtype=jnp.int32)[None, :] < (TRUNC + 1 - own_waves)[:, None]
    keeper = keeper[:, None, :]
    blank = jnp.zeros_like(flat_spec)
    doubled = jnp.stack(
        [jnp.where(keeper, flat_spec, blank), jnp.where(keeper, blank, flat_spec)], axis=1
    )
    fourier = jnp.einsum("pwcn,pln->pwcl", doubled, legendre, preferred_element_type=jnp.float32)
    fourier = fourier.astype(jnp.bfloat16).reshape(pair_dev, 2, 2, 3, level_dev, row_total)
    by_rows = lax.all_to_all(fourier, "wave", split_axis=5, concat_axis=0, tiled=True)
    whole = lax.all_gather(by_rows, "lon", axis=4, tiled=True)
    whole = jnp.transpose(whole[..., 0], (2, 3, 4, 1, 0)).reshape(2, 3 * levels, 2 * pairs)
    blocks = width // LANES
    modes = 2 * pairs
    vmem = pl.BlockSpec(memory_space=pltpu.VMEM)
    result = pl.pallas_call(
        functools.partial(row_kernel, seg_count),
        out_shape=jax.ShapeDtypeStruct((3, levels, width), jnp.bfloat16),
        in_specs=[pl.BlockSpec(memory_space=pltpu.SMEM)] + [vmem] * 4,
        out_specs=vmem,
        scratch_shapes=[
            pltpu.VMEM((SPAN, 2 * modes), jnp.bfloat16),
            pltpu.VMEM((16, modes), jnp.float32),
            pltpu.VMEM((16, modes), jnp.float32),
            pltpu.VMEM((blocks * 3 * levels, 2 * modes), jnp.float32),
            pltpu.VMEM((blocks * 3 * levels, 2 * LANES), jnp.float32),
        ],
        compiler_params=pltpu.CompilerParams(vmem_limit_bytes=40 * 1024 * 1024),
    )(
        row_lengths,
        pair_waves[None, :],
        whole,
        departure[0, :, 0, :],
        weights[:, 0, :, 0, :],
    )
    return result[:, None, :, None, :]


def solution(mesh):
    return jax.shard_map(
        local,
        mesh=mesh,
        in_specs=(
            P("wave", None, None, "lon", None),
            P("wave", None, None),
            P(),
            P("wave"),
            P("wave", None, "lon", None),
            P(None, "wave", None, "lon", None),
        ),
        out_specs=P(None, "wave", None, "lon", None),
        check_vma=False,
    )
```

time: 1390 us -> 38 us (0.03)
  local copies, waits for them, and re-layouts: 1170 us -> 3.29 us
  matrix products: 195 us -> 9.38 us
    gather x15 -> x0, local copies, waits for them, and re-layouts: 1160 us -> none  [the longest x12 1160 us: local(): jnp.take_along_axis(extended, jnp.broadcast_to(position[:, None, :, :], g...]
    dot_general x2 -> x0, matrix products: 185 us -> none  [the longest x1 98.9 us: synthesize_with(): jnp.einsum('pwfvj,jpwk->jfvk', coeffs[:, :, 1], sines, preferred_element_...]
  transfers between devices with their start and end apart: 3 -> 1, of which waited for: 2 -> 1; matrix products, arithmetic and copies ran while one was open for 0% -> 0% of each run, Pallas kernels for 0% -> 0%
where the time goes in v1:
time: 38 us; the launch traced here: 37.8 us
  matrix products  9.38 us (25%)
  starting transfers between devices  7.28 us (19%)
  waiting for transfers between devices  6.11 us (16%)
  blocking collectives  5.4 us (14%)
  local copies, waits for them, and re-layouts  3.29 us (9%)
  other arithmetic  2.78 us (7%)
  Pallas kernels  2.78 us (7%)
  between operations  0.75 us (2%)
    dot_general x1, matrix products, local(): jnp.einsum('pwcn,pln->pwcl', doubled, legendre, preferred_element_type=jn...  9.38 us
    all_to_all x1, starting transfers between devices, local(): lax.all_to_all(fourier, 'wave', split_axis=5, concat_axis=0, tiled=True)  7.28 us
    all_to_all x1, waiting for transfers between devices, local(): lax.all_to_all(fourier, 'wave', split_axis=5, concat_axis=0, tiled=True)  6.11 us
    all_gather x1, blocking collectives, local(): whole = lax.all_gather(by_rows, 'lon', axis=4, tiled=True)  5.4 us
    pallas_call x1, Pallas kernels, local(): pl.pallas_call(functools.partial(row_kernel, seg_count), out_shape=jax.Sh...  2.78 us
    unnamed x10, local copies, waits for them, and re-layouts  2.11 us
    select_n x1, other arithmetic, local(): jnp.where(keeper, flat_spec, blank)  1.76 us
    sub x1, other arithmetic, local(): TRUNC + 1 - own_waves  0.89 us
  transfers between devices with their start and end apart: 1, of which 1 were waited for; matrix products, arithmetic and copies ran while one was open for 0% of the time, Pallas kernels for 0%

profile of v1, /device:TPU:0, one launch (start us, length us, event | category | flops | bytes accessed | tf_op | source)
XLA Modules:
  0.0 37.8 jit_solution(14552905340026749538)
XLA Ops:
  0.0 0.0 copy-start
  0.0 0.9 %dynamic-slice_subtract_fusion = s32[80]{0:T(128)S(1)} fusion(s32[640]{0:T(1024)} %param.8, s32[]{:T(128)S(6)} %select_n.24), kind=kLoop, calls=%fused_computation.10 | loop fusion | flops 80 | bytes 644 | tf_op jit(solution)/shard_map/sub | solution.py:116
  0.9 0.1 iota_compare_fusion
  1.0 2.1 %copy.22 = bf16[80,2,3,2,1281]{4,0,3,2,1:T(8,128)(2,1)S(1)} copy(bf16[80,2,3,2,1281]{4,3,2,1,0:T(2,128)(2,1)} %param.6) | data formatting | bytes 4919040 | tf_op args[0]
  3.1 1.8 %copy_select_fusion.1 = (bf16[80,1,12,1281]{3,2,1,0:T(8,128)(2,1)S(1)}, bf16[80,1,12,1281]{3,2,1,0:T(8,128)(2,1)S(1)}) fusion(bf16[80,1,12,1281]{3,0,2,1:T(8,128)(2,1)S(1)} %bitcast.30, pred[80,1281]{1,0:T(8,128)(4,1)S(1)} %iota_compare_fusion), kind=kLoop, calls=%fused_computation.5 | loop fusion | flops 2459520 | bytes 7481040 | tf_op jit(solution)/shard_map/jit(_where)/select_n | solution.py:120
  4.9 0.0 copy-done
  4.9 0.0 copy-start.3
  4.9 0.0 copy-start.2
  4.9 0.0 copy-start.1
  4.9 9.4 %fusion.5 = bf16[80,2,12,8]{2,3,1,0:T(8,128)(2,1)S(1)} fusion(bf16[80,8,1281]{2,1,0:T(8,128)(2,1)S(1)} %copy-done, bf16[80,1,12,1281]{3,2,1,0:T(8,128)(2,1)S(1)} %get-tuple-element.6, bf16[80,1,12,1281]{3,2,1,0:T(8,128)(2,1)S(1)} %get-tuple-element.5), kind=kOutput, calls=%fused_computation.7 | convolution fusion | flops 41827200 | bytes 6589440 | tf_op jit(solution)/shard_map/pwcn,pln->pwcl/dot_general | solution.py:122
  14.3 0.4 copy.25
  14.7 0.7 %copy.26 = bf16[80,2,2,3,2,8]{0,4,3,2,1,5:T(2,128)(2,1)} copy(bf16[80,2,2,3,2,8]{0,5,4,3,2,1:T(8,128)(2,1)S(1)} %bitcast.33) | data formatting | bytes 61440 | tf_op jit(solution)/shard_map/reshape | solution.py:123
  15.3 7.3 %all-to-all-start = ((bf16[80,2,2,3,2,8]{0,4,3,2,1,5:T(2,128)(2,1)}), bf16[80,2,2,3,2,8]{0,4,3,2,1,5:T(2,128)(2,1)S(1)}, u32[]{:S(2)}, u32[]{:S(2)}) async-start(bf16[80,2,2,3,2,8]{0,4,3,2,1,5:T(2,128)(2,1)} %copy.26), calls=%async_computation | async-start | bytes 98304 | tf_op jit(solution)/shard_map/all_to_all | solution.py:124
  22.6 0.0 copy-done.3
  22.6 0.0 copy-done.2
  23.3 6.1 %all-to-all-done = bf16[80,2,2,3,2,8]{0,4,3,2,1,5:T(2,128)(2,1)S(1)} async-done(((bf16[80,2,2,3,2,8]{0,4,3,2,1,5:T(2,128)(2,1)}), bf16[80,2,2,3,2,8]{0,4,3,2,1,5:T(2,128)(2,1)S(1)}, u32[]{:S(2)}, u32[]{:S(2)}) %all-to-all-start) | async-done | bytes 30752 | tf_op jit(solution)/shard_map/all_to_all | solution.py:124
  29.4 0.1 reshape.50
  29.6 5.4 %all_gather.3 = bf16[640,2,2,3,8,1]{0,2,5,3,1,4:T(2,128)(2,1)S(1)} all-gather(bf16[640,2,2,3,2,1]{0,2,5,3,1,4:T(2,128)(2,1)S(1)} %reshape.50), channel_id=1, replica_groups=mesh['wave'=8,'lon'=4] {'lon'}, dimensions={4}, use_global_device_ids=true | all-gather | bytes 153600 | tf_op jit(solution)/shard_map/all_gather | solution.py:125
  35.0 0.0 copy-done.1
  35.0 2.8 %shard_map.64 = bf16[3,8,1280]{2,1,0:T(8,128)(2,1)} custom-call(s32[1]{0:T(128)S(6)} %copy.39.length_ref, s32[1,640]{1,0:T(1,128)S(1)} %broadcast_in_dim.23.pairs_ref, bf16[2,24,1280]{2,1,0:T(8,128)(2,1)S(1)} %bitcast.27, s32[8,1280]{1,0:T(8,128)S(1)} %bitcast.28, bf16[4,8,1280]{2,1,0:T(8,128)(2,1)S(1)} %bitcast.29), custom_call_target="tpu_custom_call" | custom-call | tf_op jit(solution)/shard_map/pallas_call | solution.py:130
  (4 shorter events, 0.0 us)
Async XLA Ops:
  0.0 4.9 %copy-start = (bf16[80,8,1281]{2,1,0:T(8,128)(2,1)S(1)}, bf16[80,8,1281]{2,1,0:T(8,128)(2,1)}, u32[]{:S(2)}) copy-start(bf16[80,8,1281]{2,1,0:T(8,128)(2,1)} %param.7) | copy-start | bytes 4919044
  4.9 17.7 %copy-start.3 = (s32[640]{0:T(1024)S(1)}, s32[640]{0:T(1024)}, u32[]{:S(2)}) copy-start(s32[640]{0:T(1024)} %param.8) | copy-start | bytes 7684
  4.9 17.7 %copy-start.2 = (s32[1,8,1,1280]{3,2,1,0:T(1,128)S(1)}, s32[1,8,1,1280]{3,2,1,0:T(1,128)}, u32[]{:S(2)}) copy-start(s32[1,8,1,1280]{3,2,1,0:T(1,128)} %param.10) | copy-start | bytes 122884
  4.9 30.1 %copy-start.1 = (bf16[4,1,8,1,1280]{4,2,3,1,0:T(8,128)(2,1)S(1)}, bf16[4,1,8,1,1280]{4,2,3,1,0:T(8,128)(2,1)}, u32[]{:S(2)}) copy-start(bf16[4,1,8,1,1280]{4,2,3,1,0:T(8,128)(2,1)} %param.11) | copy-start | bytes 245764
  15.3 14.1 %all-to-all-start = ((bf16[80,2,2,3,2,8]{0,4,3,2,1,5:T(2,128)(2,1)}), bf16[80,2,2,3,2,8]{0,4,3,2,1,5:T(2,128)(2,1)S(1)}, u32[]{:S(2)}, u32[]{:S(2)}) async-start(bf16[80,2,2,3,2,8]{0,4,3,2,1,5:T(2,128)(2,1)} %copy.26), calls=%async_computation | async-start | bytes 98304 | tf_op jit(solution)/shard_map/all_to_all | solution.py:124

commit v2 on v1

--- a/solution.py
+++ b/solution.py
@@ -3,6 +3,7 @@
 
 import jax
 import jax.numpy as jnp
+import numpy as np
 from jax import lax
 from jax.experimental import pallas as pl
 from jax.experimental.pallas import tpu as pltpu
@@ -87,18 +88,91 @@
             out_ref[f, :, lanes] = kept.astype(jnp.bfloat16)
 
 
+def exchange(send_ref, recv_ref, send_sem, recv_sem):
+    along = lax.axis_size("lon")
+    total = lax.axis_size("wave") * along
+    me = lax.axis_index("wave") * along + lax.axis_index("lon")
+
+    def target_of(step):
+        target = lax.rem(me + step, total)
+        return lax.div(target, along), lax.rem(target, along)
+
+    def copy_at(step):
+        row, place = target_of(step)
+        return pltpu.make_async_remote_copy(
+            src_ref=send_ref.at[row],
+            dst_ref=recv_ref.at[me],
+            send_sem=send_sem.at[step],
+            recv_sem=recv_sem.at[step],
+            device_id=(row, place),
+            device_id_type=pl.DeviceIdType.MESH,
+        )
+
+    def greet():
+        barrier = pltpu.get_barrier_semaphore()
+
+        def one(step, carry):
+            pl.semaphore_signal(
+                barrier, inc=1, device_id=target_of(step), device_id_type=pl.DeviceIdType.MESH
+            )
+            return carry
+
+        lax.fori_loop(1, total, one, 0)
+
+    def start():
+        pl.semaphore_wait(pltpu.get_barrier_semaphore(), total - 1)
+
+        def one(step, carry):
+            copy_at(step).start()
+            return carry
+
+        lax.fori_loop(1, total, one, 0)
+        recv_ref[me] = send_ref[lax.axis_index("wave")]
+
+    def finish():
+        def one(step, carry):
+            copy_at(step).wait()
+            return carry
+
+        lax.fori_loop(1, total, one, 0)
+
+    return greet, start, finish
+
+
 def row_kernel(
-    seg_count, length_ref, pairs_ref, fourier_ref, departure_ref, weights_ref, out_ref,
-    table_ref, start_cos, start_sin, lhs_ref, grid_ref,
+    seg_count, length_ref, pairs_ref, send_ref, order_ref, departure_ref, weights_ref, out_ref,
+    table_ref, start_cos, start_sin, lhs_ref, grid_ref, recv_ref, fourier_ref, send_sem, recv_sem,
 ):
     length = length_ref[0]
     levels, width = departure_ref.shape
     blocks = width // LANES
+    greet, start, finish = exchange(send_ref, recv_ref, send_sem, recv_sem)
+    greet()
+    start()
     make_tables(seg_count, pairs_ref, length, table_ref, start_cos, start_sin)
-    real = fourier_ref[0].astype(jnp.float32)
-    imag = fourier_ref[1].astype(jnp.float32)
+    finish()
+    along = lax.axis_size("lon")
+    waves = lax.axis_size("wave")
+    pair_dev = pairs_ref.shape[1] // waves
+    for i in range(waves):
+        parts = jnp.concatenate([recv_ref[i * along + g] for g in range(along)], axis=0)
+        ordered = jnp.dot(order_ref[...], parts, preferred_element_type=jnp.float32)
+        for s in range(2):
+            at = (s * waves + i) * pair_dev
+            fourier_ref[:, at : at + pair_dev] = ordered[:, s * pair_dev : (s + 1) * pair_dev]
+    real = fourier_ref[: 3 * levels]
+    imag = fourier_ref[3 * levels :]
     synthesize(real, imag, blocks, table_ref, start_cos, start_sin, lhs_ref, grid_ref)
     depart(length // seg_count, blocks, levels, departure_ref, weights_ref, grid_ref, out_ref)
+
+
+def row_order(levels, level_dev, chunk):
+    order = np.zeros((6 * levels, levels // level_dev * chunk), np.float32)
+    for part_field in range(6):
+        for v in range(levels):
+            source = v // level_dev * chunk + part_field * level_dev + v % level_dev
+            order[part_field * levels + v, source] = 1.0
+    return jnp.asarray(order, jnp.bfloat16)
 
 
 def local(spectra, legendre, pair_waves, row_lengths, departure, weights):
@@ -120,17 +194,18 @@
         [jnp.where(keeper, flat_spec, blank), jnp.where(keeper, blank, flat_spec)], axis=1
     )
     fourier = jnp.einsum("pwcn,pln->pwcl", doubled, legendre, preferred_element_type=jnp.float32)
-    fourier = fourier.astype(jnp.bfloat16).reshape(pair_dev, 2, 2, 3, level_dev, row_total)
-    by_rows = lax.all_to_all(fourier, "wave", split_axis=5, concat_axis=0, tiled=True)
-    whole = lax.all_gather(by_rows, "lon", axis=4, tiled=True)
-    whole = jnp.transpose(whole[..., 0], (2, 3, 4, 1, 0)).reshape(2, 3 * levels, 2 * pairs)
+    chunk = -(-columns // 16) * 16
+    send = jnp.transpose(fourier.astype(jnp.bfloat16), (3, 2, 1, 0))
+    send = send.reshape(row_total, columns, 2 * pair_dev)
+    send = jnp.pad(send, ((0, 0), (0, chunk - columns), (0, 0)))
+    devices = lax.axis_size("wave") * seg_count
     blocks = width // LANES
     modes = 2 * pairs
     vmem = pl.BlockSpec(memory_space=pltpu.VMEM)
     result = pl.pallas_call(
         functools.partial(row_kernel, seg_count),
         out_shape=jax.ShapeDtypeStruct((3, levels, width), jnp.bfloat16),
-        in_specs=[pl.BlockSpec(memory_space=pltpu.SMEM)] + [vmem] * 4,
+        in_specs=[pl.BlockSpec(memory_space=pltpu.SMEM)] + [vmem] * 5,
         out_specs=vmem,
         scratch_shapes=[
             pltpu.VMEM((SPAN, 2 * modes), jnp.bfloat16),
@@ -138,12 +213,19 @@
             pltpu.VMEM((16, modes), jnp.float32),
             pltpu.VMEM((blocks * 3 * levels, 2 * modes), jnp.float32),
             pltpu.VMEM((blocks * 3 * levels, 2 * LANES), jnp.float32),
+            pltpu.VMEM((devices, chunk, 2 * pair_dev), jnp.bfloat16),
+            pltpu.VMEM((6 * levels, modes), jnp.float32),
+            pltpu.SemaphoreType.DMA((devices,)),
+            pltpu.SemaphoreType.DMA((devices,)),
         ],
-        compiler_params=pltpu.CompilerParams(vmem_limit_bytes=40 * 1024 * 1024),
+        compiler_params=pltpu.CompilerParams(
+            vmem_limit_bytes=40 * 1024 * 1024, collective_id=0, has_side_effects=True
+        ),
     )(
         row_lengths,
         pair_waves[None, :],
-        whole,
+        send,
+        row_order(levels, level_dev, chunk),
         departure[0, :, 0, :],
         weights[:, 0, :, 0, :],
     )

time: 38 us -> 30.7 us (0.81)
  Pallas kernels: 2.78 us -> 14.2 us
  starting transfers between devices: 7.28 us -> 0 us
  waiting for transfers between devices: 6.11 us -> 0 us
  blocking collectives: 5.4 us -> 0 us
    pallas_call x1, Pallas kernels: 2.78 us -> 14.2 us  [local(): pl.pallas_call(functools.partial(row_kernel, seg_count), out_shape=jax.Sh...]
    all_to_all x1 -> x0, starting transfers between devices: 7.28 us -> none  [local(): lax.all_to_all(fourier, 'wave', split_axis=5, concat_axis=0, tiled=True)]
    all_to_all x1 -> x0, waiting for transfers between devices: 6.11 us -> none  [local(): lax.all_to_all(fourier, 'wave', split_axis=5, concat_axis=0, tiled=True)]
    all_gather x1 -> x0, blocking collectives: 5.4 us -> none  [local(): whole = lax.all_gather(by_rows, 'lon', axis=4, tiled=True)]
    unnamed x10 -> x13, local copies, waits for them, and re-layouts: 2.11 us -> 2.74 us
  transfers between devices with their start and end apart: 1 -> 0, of which waited for: 1 -> 0; matrix products, arithmetic and copies ran while one was open for 0% -> 0% of each run, Pallas kernels for 0% -> 0%
where the time goes in v2:
time: 30.7 us; the launch traced here: 30.4 us
  Pallas kernels  14.2 us (46%)
  matrix products  9.38 us (31%)
  local copies, waits for them, and re-layouts  3.22 us (10%)
  other arithmetic  2.78 us (9%)
  between operations  0.78 us (3%)
    pallas_call x1, Pallas kernels, local(): pl.pallas_call(functools.partial(row_kernel, seg_count), out_shape=jax.Sh...  14.2 us
    dot_general x1, matrix products, local(): jnp.einsum('pwcn,pln->pwcl', doubled, legendre, preferred_element_type=jn...  9.38 us
    unnamed x13, local copies, waits for them, and re-layouts  2.74 us
    select_n x1, other arithmetic, local(): jnp.where(keeper, flat_spec, blank)  1.76 us
    sub x1, other arithmetic, local(): TRUNC + 1 - own_waves  0.89 us

profile of v2, /device:TPU:0, one launch (start us, length us, event | category | flops | bytes accessed | tf_op | source)
XLA Modules:
  0.0 30.4 jit_solution(4603155691671241318)
XLA Ops:
  0.0 0.0 copy-start
  0.0 0.9 %dynamic-slice_subtract_fusion = s32[80]{0:T(128)S(1)} fusion(s32[640]{0:T(1024)} %param.9, s32[]{:T(128)S(6)} %select_n.24), kind=kLoop, calls=%fused_computation.11 | loop fusion | flops 80 | bytes 644 | tf_op jit(solution)/shard_map/sub | solution.py:190
  0.9 0.1 iota_compare_fusion
  1.0 2.1 %copy.10 = bf16[80,2,3,2,1281]{4,0,3,2,1:T(8,128)(2,1)S(1)} copy(bf16[80,2,3,2,1281]{4,3,2,1,0:T(2,128)(2,1)} %param.7) | data formatting | bytes 4919040 | tf_op args[0]
  3.1 1.8 %copy_select_fusion.1 = (bf16[80,1,12,1281]{3,2,1,0:T(8,128)(2,1)S(1)}, bf16[80,1,12,1281]{3,2,1,0:T(8,128)(2,1)S(1)}) fusion(bf16[80,1,12,1281]{3,0,2,1:T(8,128)(2,1)S(1)} %bitcast.22, pred[80,1281]{1,0:T(8,128)(4,1)S(1)} %iota_compare_fusion), kind=kLoop, calls=%fused_computation.5 | loop fusion | flops 2459520 | bytes 7481040 | tf_op jit(solution)/shard_map/jit(_where)/select_n | solution.py:194
  4.9 0.0 copy-done
  4.9 0.0 copy-start.3
  4.9 0.0 copy-start.4
  4.9 0.0 copy-start.1
  4.9 0.0 copy-start.2
  4.9 9.4 %fusion.10 = bf16[8,12,2,80]{1,0,2,3:T(8,128)(2,1)S(1)} fusion(bf16[80,8,1281]{2,1,0:T(8,128)(2,1)S(1)} %copy-done, bf16[80,1,12,1281]{3,2,1,0:T(8,128)(2,1)S(1)} %get-tuple-element.6, bf16[80,1,12,1281]{3,2,1,0:T(8,128)(2,1)S(1)} %get-tuple-element.5), kind=kOutput, calls=%fused_computation.8 | convolution fusion | flops 41827200 | bytes 6589440 | tf_op jit(solution)/shard_map/pwcn,pln->pwcl/dot_general | solution.py:196
  14.3 0.4 %copy.17 = bf16[8,12,2,80]{3,2,1,0:T(2,128)(2,1)S(1)} copy(bf16[8,12,2,80]{1,0,2,3:T(8,128)(2,1)S(1)} %fusion.10) | data formatting | bytes 61440 | tf_op jit(solution)/shard_map/reshape | solution.py:199
  14.7 0.1 reshape.46
  14.8 0.0 copy-done.3
  14.8 0.0 copy-done.4
  15.5 0.0 copy-done.1
  15.5 0.0 copy-done.2
  15.5 14.2 %shard_map.73 = bf16[3,8,1280]{2,1,0:T(8,128)(2,1)S(1)} custom-call(s32[1]{0:T(128)S(6)} %copy.25.length_ref, s32[1,640]{1,0:T(1,128)S(1)} %broadcast_in_dim.23.pairs_ref, bf16[8,16,160]{2,1,0:T(8,128)(2,1)S(1)} %pad.4.send_ref, bf16[48,64]{1,0:T(8,128)(2,1)S(1)} %copy-done.2, s32[8,1280]{1,0:T(8,128)S(1)} %bitcast.20, bf16[4,8,1280]{2,1,0:T(8,128)(2,1)S(1)} %bitcast.21), custom_call_target="tpu_custom_call" | custom-call | tf_op jit(solution)/shard_map/pallas_call | solution.py:205
  29.7 0.6 %copy.26 = bf16[3,1,8,1,1280]{4,2,3,1,0:T(8,128)(2,1)} copy(bf16[3,1,8,1,1280]{4,2,3,1,0:T(8,128)(2,1)S(1)} %bitcast.19) | data formatting | bytes 122880
  (3 shorter events, 0.0 us)
Async XLA Ops:
  0.0 4.9 %copy-start = (bf16[80,8,1281]{2,1,0:T(8,128)(2,1)S(1)}, bf16[80,8,1281]{2,1,0:T(8,128)(2,1)}, u32[]{:S(2)}) copy-start(bf16[80,8,1281]{2,1,0:T(8,128)(2,1)} %param.8) | copy-start | bytes 4919044
  4.9 9.9 %copy-start.3 = (s32[1,8,1,1280]{3,2,1,0:T(1,128)S(1)}, s32[1,8,1,1280]{3,2,1,0:T(1,128)}, u32[]{:S(2)}) copy-start(s32[1,8,1,1280]{3,2,1,0:T(1,128)} %param.11) | copy-start | bytes 122884
  4.9 9.9 %copy-start.4 = (s32[640]{0:T(1024)S(1)}, s32[640]{0:T(1024)}, u32[]{:S(2)}) copy-start(s32[640]{0:T(1024)} %param.9) | copy-start | bytes 7684
  4.9 10.6 %copy-start.1 = (bf16[4,1,8,1,1280]{4,2,3,1,0:T(8,128)(2,1)S(1)}, bf16[4,1,8,1,1280]{4,2,3,1,0:T(8,128)(2,1)}, u32[]{:S(2)}) copy-start(bf16[4,1,8,1,1280]{4,2,3,1,0:T(8,128)(2,1)} %param.12) | copy-start | bytes 245764
  4.9 10.6 %copy-start.2 = (bf16[48,64]{1,0:T(8,128)(2,1)S(1)}, bf16[48,64]{1,0:T(8,128)(2,1)}, u32[]{:S(2)}) copy-start(bf16[48,64]{1,0:T(8,128)(2,1)} %constant.19.clone.order_ref) | copy-start | bytes 18436

commit v3 on v2

--- a/solution.py
+++ b/solution.py
@@ -12,6 +12,7 @@
 TRUNC = 1279
 HALO = 8
 LANES = 128
+GROUP = 16
 SHIFTS = 2 * HALO + 1
 SPAN = LANES + 2 * HALO
 
@@ -166,6 +167,61 @@
     depart(length // seg_count, blocks, levels, departure_ref, weights_ref, grid_ref, out_ref)
 
 
+def legendre_kernel(
+    pair_dev, pairs_ref, spectra_ref, legendre_ref, spread_ref, send_ref, rhs_ref, send_f
+):
+    columns, padded, packed = spectra_ref.shape
+    row_total = legendre_ref.shape[1]
+    chunk = send_ref.shape[1]
+    start = lax.axis_index("wave") * pair_dev
+    lane = lax.broadcasted_iota(jnp.int32, (row_total, packed), 1)
+    zero = jnp.zeros((row_total, packed), jnp.float32)
+    wide = 2 * GROUP * row_total
+    own = lax.broadcasted_iota(jnp.int32, (GROUP, wide), 0)
+    other = lax.broadcasted_iota(jnp.int32, (GROUP, wide), 1)
+    low = jnp.where(other >= wide // 2, other - wide // 2, other) - own * row_total
+    mine = jnp.where((low >= 0) & (low < row_total), 1.0, 0.0)[None]
+    send_f[...] = jnp.zeros_like(send_f)
+    for g in range(padded // GROUP):
+        for p in range(0, GROUP, 2):
+            first, second = [], []
+            for at in (g * GROUP + p, g * GROUP + p + 1):
+                if at < pair_dev:
+                    rows = legendre_ref[at].astype(jnp.float32)
+                    keep = lane < TRUNC + 1 - pairs_ref[start + at]
+                    first.append(jnp.where(keep, rows, 0.0))
+                    second.append(jnp.where(keep, 0.0, rows))
+                else:
+                    first.append(zero)
+                    second.append(zero)
+            for s, part in enumerate((first, second)):
+                at = (s * GROUP + p) * row_total
+                part = jnp.concatenate(part, axis=0).astype(jnp.bfloat16)
+                rhs_ref[g, at : at + 2 * row_total] = part
+        lhs = spectra_ref[:, g * GROUP : (g + 1) * GROUP, :].reshape(columns * GROUP, packed)
+        cross = lax.dot_general(
+            lhs, rhs_ref[g], (((1,), (1,)), ((), ())), preferred_element_type=jnp.float32
+        )
+        sums = jnp.sum(cross.reshape(columns, GROUP, wide) * mine, axis=1).astype(jnp.bfloat16)
+        by_row = jnp.dot(sums, spread_ref[...], preferred_element_type=jnp.float32)
+        valid = min(GROUP, pair_dev - g * GROUP)
+        for j in range(row_total):
+            for s in range(2):
+                source = (j * 2 + s) * GROUP
+                to = s * pair_dev + g * GROUP
+                send_f[j, :columns, to : to + valid] = by_row[:, source : source + valid]
+    for j in range(row_total):
+        send_ref[j] = send_f[j].astype(jnp.bfloat16)
+
+
+def lane_order(row_total):
+    wide = 2 * GROUP * row_total
+    source = np.arange(wide).reshape(2, GROUP, row_total).transpose(2, 0, 1).reshape(-1)
+    order = np.zeros((wide, wide), np.float32)
+    order[source, np.arange(wide)] = 1.0
+    return jnp.asarray(order, jnp.bfloat16)
+
+
 def row_order(levels, level_dev, chunk):
     order = np.zeros((6 * levels, levels // level_dev * chunk), np.float32)
     for part_field in range(6):
@@ -184,28 +240,31 @@
     levels, width = departure.shape[1], departure.shape[3]
     seg_count = lax.axis_size("lon")
     columns = 6 * level_dev
-    start_pair = lax.axis_index("wave") * pair_dev
-    own_waves = lax.dynamic_slice_in_dim(pair_waves, start_pair, pair_dev)
-    flat_spec = spectra.reshape(pair_dev, columns, packed)
-    keeper = jnp.arange(packed, dtype=jnp.int32)[None, :] < (TRUNC + 1 - own_waves)[:, None]
-    keeper = keeper[:, None, :]
-    blank = jnp.zeros_like(flat_spec)
-    doubled = jnp.stack(
-        [jnp.where(keeper, flat_spec, blank), jnp.where(keeper, blank, flat_spec)], axis=1
-    )
-    fourier = jnp.einsum("pwcn,pln->pwcl", doubled, legendre, preferred_element_type=jnp.float32)
+    padded = -(-pair_dev // GROUP) * GROUP
     chunk = -(-columns // 16) * 16
-    send = jnp.transpose(fourier.astype(jnp.bfloat16), (3, 2, 1, 0))
-    send = send.reshape(row_total, columns, 2 * pair_dev)
-    send = jnp.pad(send, ((0, 0), (0, chunk - columns), (0, 0)))
+    flat_spec = jnp.transpose(spectra, (1, 2, 3, 0, 4)).reshape(columns, pair_dev, packed)
+    flat_spec = jnp.pad(flat_spec, ((0, 0), (0, padded - pair_dev), (0, 0)))
+    vmem = pl.BlockSpec(memory_space=pltpu.VMEM)
+    smem = pl.BlockSpec(memory_space=pltpu.SMEM)
+    wide = 2 * GROUP * row_total
+    send = pl.pallas_call(
+        functools.partial(legendre_kernel, pair_dev),
+        out_shape=jax.ShapeDtypeStruct((row_total, chunk, 2 * pair_dev), jnp.bfloat16),
+        in_specs=[smem] + [vmem] * 3,
+        out_specs=vmem,
+        scratch_shapes=[
+            pltpu.VMEM((padded // GROUP, wide, packed), jnp.bfloat16),
+            pltpu.VMEM((row_total, chunk, 2 * pair_dev), jnp.float32),
+        ],
+        compiler_params=pltpu.CompilerParams(vmem_limit_bytes=40 * 1024 * 1024),
+    )(pair_waves, flat_spec, legendre, lane_order(row_total))
     devices = lax.axis_size("wave") * seg_count
     blocks = width // LANES
     modes = 2 * pairs
-    vmem = pl.BlockSpec(memory_space=pltpu.VMEM)
     result = pl.pallas_call(
         functools.partial(row_kernel, seg_count),
         out_shape=jax.ShapeDtypeStruct((3, levels, width), jnp.bfloat16),
-        in_specs=[pl.BlockSpec(memory_space=pltpu.SMEM)] + [vmem] * 5,
+        in_specs=[smem] + [vmem] * 5,
         out_specs=vmem,
         scratch_shapes=[
             pltpu.VMEM((SPAN, 2 * modes), jnp.bfloat16),

time: 30.7 us -> 21.5 us (0.70)
  matrix products: 9.38 us -> 0 us
  Pallas kernels: 14.2 us -> 17.5 us
  other arithmetic: 2.78 us -> 0 us
    dot_general x1 -> x0, matrix products: 9.38 us -> none  [local(): jnp.einsum('pwcn,pln->pwcl', doubled, legendre, preferred_element_type=jn...]
    pallas_call x0 -> x1, Pallas kernels: none -> 3.32 us  [local(): pl.pallas_call(functools.partial(legendre_kernel, pair_dev), out_shape=ja...]
    transpose x0 -> x1, local copies, waits for them, and re-layouts: none -> 2.22 us  [local(): jnp.transpose(spectra, (1, 2, 3, 0, 4)).reshape(columns, pair_dev, packed)]
    unnamed x13 -> x14, local copies, waits for them, and re-layouts: 2.74 us -> 0.7 us
    select_n x1 -> x0, other arithmetic: 1.76 us -> none  [local(): jnp.where(keeper, flat_spec, blank)]
    sub x1 -> x0, other arithmetic: 0.89 us -> none  [local(): TRUNC + 1 - own_waves]
    reshape x2 -> x0, local copies, waits for them, and re-layouts: 0.46 us -> none  [local(): send = send.reshape(row_total, columns, 2 * pair_dev)]
where the time goes in v3:
time: 21.5 us; the launch traced here: 21.2 us
  Pallas kernels  17.5 us (81%)
  local copies, waits for them, and re-layouts  2.92 us (14%)
  between operations  0.73 us (3%)
    pallas_call x1, Pallas kernels, local(): pl.pallas_call(functools.partial(row_kernel, seg_count), out_shape=jax.Sh...  14.2 us
    pallas_call x1, Pallas kernels, local(): pl.pallas_call(functools.partial(legendre_kernel, pair_dev), out_shape=ja...  3.32 us
    transpose x1, local copies, waits for them, and re-layouts, local(): jnp.transpose(spectra, (1, 2, 3, 0, 4)).reshape(columns, pair_dev, packed)  2.22 us
    unnamed x14, local copies, waits for them, and re-layouts  0.7 us

profile of v3, /device:TPU:0, one launch (start us, length us, event | category | flops | bytes accessed | tf_op | source)
XLA Modules:
  0.0 21.2 jit_solution(17722937700749620838)
XLA Ops:
  0.0 0.0 copy-start
  0.0 0.0 copy-start.1
  0.0 0.0 copy-start.3
  0.0 2.2 %copy.9 = bf16[2,3,2,80,1281]{4,3,2,1,0:T(8,128)(2,1)S(1)} copy(bf16[2,3,2,80,1281]{4,2,1,0,3:T(2,128)(2,1)} %bitcast.13) | data formatting | bytes 4919040 | tf_op jit(solution)/shard_map/transpose | solution.py:245
  2.2 0.0 copy-start.5
  2.2 0.0 copy-start.2
  2.2 0.0 copy-start.4
  2.3 0.0 copy-done
  2.3 0.0 copy-done.1
  2.3 0.0 copy-done.3
  2.3 3.3 %shard_map.82.send_ref = bf16[8,16,160]{2,1,0:T(8,128)(2,1)S(1)} custom-call(s32[640]{0:T(1024)S(1)} %copy-done.3, bf16[12,80,1281]{2,1,0:T(8,128)(2,1)S(1)} %bitcast.9, bf16[80,8,1281]{2,1,0:T(8,128)(2,1)S(1)} %copy-done, bf16[256,256]{1,0:T(8,128)(2,1)S(1)} %copy-done.1), custom_call_target="tpu_custom_call" | custom-call | tf_op jit(solution)/shard_map/pallas_call | solution.py:250
  5.6 0.0 copy-done.5
  6.3 0.0 copy-done.2
  6.3 0.0 copy-done.4
  6.3 14.2 %shard_map.83 = bf16[3,8,1280]{2,1,0:T(8,128)(2,1)S(1)} custom-call(s32[1]{0:T(128)S(6)} %copy.15.length_ref, s32[1,640]{1,0:T(1,128)S(1)} %broadcast_in_dim.6.pairs_ref, bf16[8,16,160]{2,1,0:T(8,128)(2,1)S(1)} %shard_map.82.send_ref, bf16[48,64]{1,0:T(8,128)(2,1)S(1)} %copy-done.4, s32[8,1280]{1,0:T(8,128)S(1)} %bitcast.11, bf16[4,8,1280]{2,1,0:T(8,128)(2,1)S(1)} %bitcast.12), custom_call_target="tpu_custom_call" | custom-call | tf_op jit(solution)/shard_map/pallas_call | solution.py:264
  20.5 0.6 %copy.16 = bf16[3,1,8,1,1280]{4,2,3,1,0:T(8,128)(2,1)} copy(bf16[3,1,8,1,1280]{4,2,3,1,0:T(8,128)(2,1)S(1)} %bitcast.10) | data formatting | bytes 122880
  (2 shorter events, 0.0 us)
Async XLA Ops:
  0.0 2.3 %copy-start = (bf16[80,8,1281]{2,1,0:T(8,128)(2,1)S(1)}, bf16[80,8,1281]{2,1,0:T(8,128)(2,1)}, u32[]{:S(2)}) copy-start(bf16[80,8,1281]{2,1,0:T(8,128)(2,1)} %legendre_ref.1) | copy-start | bytes 4919044
  0.0 2.3 %copy-start.1 = (bf16[256,256]{1,0:T(8,128)(2,1)S(1)}, bf16[256,256]{1,0:T(8,128)(2,1)}, u32[]{:S(2)}) copy-start(bf16[256,256]{1,0:T(8,128)(2,1)} %constant.2.clone.spread_ref) | copy-start | bytes 393220
  0.0 2.3 %copy-start.3 = (s32[640]{0:T(1024)S(1)}, s32[640]{0:T(1024)}, u32[]{:S(2)}) copy-start(s32[640]{0:T(1024)} %pairs_ref.1) | copy-start | bytes 7684
  2.2 3.4 %copy-start.5 = (s32[1,8,1,1280]{3,2,1,0:T(1,128)S(1)}, s32[1,8,1,1280]{3,2,1,0:T(1,128)}, u32[]{:S(2)}) copy-start(s32[1,8,1,1280]{3,2,1,0:T(1,128)} %param.12) | copy-start | bytes 122884
  2.2 4.1 %copy-start.2 = (bf16[4,1,8,1,1280]{4,2,3,1,0:T(8,128)(2,1)S(1)}, bf16[4,1,8,1,1280]{4,2,3,1,0:T(8,128)(2,1)}, u32[]{:S(2)}) copy-start(bf16[4,1,8,1,1280]{4,2,3,1,0:T(8,128)(2,1)} %param.13) | copy-start | bytes 245764
  2.2 4.1 %copy-start.4 = (bf16[48,64]{1,0:T(8,128)(2,1)S(1)}, bf16[48,64]{1,0:T(8,128)(2,1)}, u32[]{:S(2)}) copy-start(bf16[48,64]{1,0:T(8,128)(2,1)} %constant.6.clone.order_ref) | copy-start | bytes 18436

commit v4 on v3

--- a/solution.py
+++ b/solution.py
@@ -89,65 +89,95 @@
             out_ref[f, :, lanes] = kept.astype(jnp.bfloat16)
 
 
-def exchange(send_ref, recv_ref, send_sem, recv_sem):
-    along = lax.axis_size("lon")
-    total = lax.axis_size("wave") * along
-    me = lax.axis_index("wave") * along + lax.axis_index("lon")
-
-    def target_of(step):
-        target = lax.rem(me + step, total)
-        return lax.div(target, along), lax.rem(target, along)
-
-    def copy_at(step):
-        row, place = target_of(step)
+def exchange(send_ref, recv_ref, send_sems, recv_sems):
+    rows = lax.axis_size("wave")
+    chips = lax.axis_size("lon") // 2
+    row, place = lax.axis_index("wave"), lax.axis_index("lon")
+    chip, core = lax.div(place, 2), lax.rem(place, 2)
+
+    def remote(phase, slot, source, to, device):
         return pltpu.make_async_remote_copy(
-            src_ref=send_ref.at[row],
-            dst_ref=recv_ref.at[me],
-            send_sem=send_sem.at[step],
-            recv_sem=recv_sem.at[step],
-            device_id=(row, place),
+            src_ref=source,
+            dst_ref=to,
+            send_sem=send_sems[phase].at[slot],
+            recv_sem=recv_sems[phase].at[slot],
+            device_id=device,
             device_id_type=pl.DeviceIdType.MESH,
         )
 
+    def along_wave(step):
+        target = lax.rem(row + step, rows)
+        return remote(
+            0, step, send_ref.at[target], recv_ref.at[place, row], (target, place)
+        )
+
+    def chip_at(step):
+        return (row, lax.rem(chip + step, chips) * 2 + core)
+
+    def along_chips(step, away):
+        maker = lax.rem(row + rows - step, rows)
+        block = recv_ref.at[place, maker]
+        return remote(1, away * rows + step, block, block, chip_at(away))
+
+    def to_sibling(away):
+        block = recv_ref.at[lax.rem(chip + chips - away, chips) * 2 + core]
+        return remote(2, away, block, block, (row, chip * 2 + 1 - core))
+
+    def loop(first, last, body):
+        def one(step, carry):
+            body(step)
+            return carry
+
+        lax.fori_loop(first, last, one, 0)
+
     def greet():
         barrier = pltpu.get_barrier_semaphore()
 
-        def one(step, carry):
+        def signal(device):
             pl.semaphore_signal(
-                barrier, inc=1, device_id=target_of(step), device_id_type=pl.DeviceIdType.MESH
+                barrier, inc=1, device_id=device, device_id_type=pl.DeviceIdType.MESH
             )
-            return carry
-
-        lax.fori_loop(1, total, one, 0)
+
+        loop(1, rows, lambda step: signal((lax.rem(row + step, rows), place)))
+        for away in range(1, chips):
+            signal(chip_at(away))
+        signal((row, chip * 2 + 1 - core))
 
     def start():
-        pl.semaphore_wait(pltpu.get_barrier_semaphore(), total - 1)
-
-        def one(step, carry):
-            copy_at(step).start()
-            return carry
-
-        lax.fori_loop(1, total, one, 0)
-        recv_ref[me] = send_ref[lax.axis_index("wave")]
+        pl.semaphore_wait(pltpu.get_barrier_semaphore(), rows + chips - 1)
+        loop(1, rows, lambda step: along_wave(step).start())
+        recv_ref[place, row] = send_ref[row]
+        for away in range(1, chips):
+            along_chips(0, away).start()
 
     def finish():
-        def one(step, carry):
-            copy_at(step).wait()
-            return carry
-
-        lax.fori_loop(1, total, one, 0)
+        def pass_on(step):
+            along_wave(step).wait_recv()
+            for away in range(1, chips):
+                along_chips(step, away).start()
+
+        loop(1, rows, pass_on)
+        to_sibling(0).start()
+        for away in range(1, chips):
+            loop(0, rows, lambda step: along_chips(step, away).wait_recv())
+            to_sibling(away).start()
+        for away in range(chips):
+            to_sibling(away).wait()
+        loop(1, rows, lambda step: along_wave(step).wait_send())
+        for away in range(1, chips):
+            loop(0, rows, lambda step: along_chips(step, away).wait_send())
 
     return greet, start, finish
 
 
 def row_kernel(
     seg_count, length_ref, pairs_ref, send_ref, order_ref, departure_ref, weights_ref, out_ref,
-    table_ref, start_cos, start_sin, lhs_ref, grid_ref, recv_ref, fourier_ref, send_sem, recv_sem,
+    table_ref, start_cos, start_sin, lhs_ref, grid_ref, recv_ref, fourier_ref, *sems,
 ):
     length = length_ref[0]
     levels, width = departure_ref.shape
     blocks = width // LANES
-    greet, start, finish = exchange(send_ref, recv_ref, send_sem, recv_sem)
+    greet, start, finish = exchange(send_ref, recv_ref, sems[:3], sems[3:])
     greet()
     start()
     make_tables(seg_count, pairs_ref, length, table_ref, start_cos, start_sin)
@@ -156,7 +186,7 @@
     waves = lax.axis_size("wave")
     pair_dev = pairs_ref.shape[1] // waves
     for i in range(waves):
-        parts = jnp.concatenate([recv_ref[i * along + g] for g in range(along)], axis=0)
+        parts = jnp.concatenate([recv_ref[g, i] for g in range(along)], axis=0)
         ordered = jnp.dot(order_ref[...], parts, preferred_element_type=jnp.float32)
         for s in range(2):
             at = (s * waves + i) * pair_dev
@@ -258,7 +288,8 @@
         ],
         compiler_params=pltpu.CompilerParams(vmem_limit_bytes=40 * 1024 * 1024),
     )(pair_waves, flat_spec, legendre, lane_order(row_total))
-    devices = lax.axis_size("wave") * seg_count
+    rows = lax.axis_size("wave")
+    counts = (rows, seg_count // 2 * rows, seg_count // 2)
     blocks = width // LANES
     modes = 2 * pairs
     result = pl.pallas_call(
@@ -272,11 +303,10 @@
             pltpu.VMEM((16, modes), jnp.float32),
             pltpu.VMEM((blocks * 3 * levels, 2 * modes), jnp.float32),
             pltpu.VMEM((blocks * 3 * levels, 2 * LANES), jnp.float32),
-            pltpu.VMEM((devices, chunk, 2 * pair_dev), jnp.bfloat16),
+            pltpu.VMEM((seg_count, rows, chunk, 2 * pair_dev), jnp.bfloat16),
             pltpu.VMEM((6 * levels, modes), jnp.float32),
-            pltpu.SemaphoreType.DMA((devices,)),
-            pltpu.SemaphoreType.DMA((devices,)),
-        ],
+        ]
+        + [pltpu.SemaphoreType.DMA((count,)) for count in counts * 2],
         compiler_params=pltpu.CompilerParams(
             vmem_limit_bytes=40 * 1024 * 1024, collective_id=0, has_side_effects=True
         ),

time: 21.5 us -> 22.4 us (1.042)
  Pallas kernels: 17.5 us -> 18.6 us
    pallas_call x1, Pallas kernels: 14.2 us -> 15.3 us  [local(): pl.pallas_call(functools.partial(row_kernel, seg_count), out_shape=jax.Sh...]
where the time goes in v4:
time: 22.4 us; the launch traced here: 22.3 us
  Pallas kernels  18.6 us (83%)
  local copies, waits for them, and re-layouts  2.92 us (13%)
  between operations  0.73 us (3%)
    pallas_call x1, Pallas kernels, local(): pl.pallas_call(functools.partial(row_kernel, seg_count), out_shape=jax.Sh...  15.3 us
    pallas_call x1, Pallas kernels, local(): pl.pallas_call(functools.partial(legendre_kernel, pair_dev), out_shape=ja...  3.32 us
    transpose x1, local copies, waits for them, and re-layouts, local(): jnp.transpose(spectra, (1, 2, 3, 0, 4)).reshape(columns, pair_dev, packed)  2.22 us
    unnamed x14, local copies, waits for them, and re-layouts  0.7 us

profile of v4, /device:TPU:0, one launch (start us, length us, event | category | flops | bytes accessed | tf_op | source)
XLA Modules:
  0.0 22.3 jit_solution(6504086176384398324)
XLA Ops:
  0.0 0.0 copy-start
  0.0 0.0 copy-start.1
  0.0 0.0 copy-start.3
  0.0 2.2 %copy.9 = bf16[2,3,2,80,1281]{4,3,2,1,0:T(8,128)(2,1)S(1)} copy(bf16[2,3,2,80,1281]{4,2,1,0,3:T(2,128)(2,1)} %bitcast.13) | data formatting | bytes 4919040 | tf_op jit(solution)/shard_map/transpose | solution.py:275
  2.2 0.0 copy-start.5
  2.2 0.0 copy-start.2
  2.2 0.0 copy-start.4
  2.3 0.0 copy-done
  2.3 0.0 copy-done.1
  2.3 0.0 copy-done.3
  2.3 3.3 %shard_map.82.send_ref = bf16[8,16,160]{2,1,0:T(8,128)(2,1)S(1)} custom-call(s32[640]{0:T(1024)S(1)} %copy-done.3, bf16[12,80,1281]{2,1,0:T(8,128)(2,1)S(1)} %bitcast.9, bf16[80,8,1281]{2,1,0:T(8,128)(2,1)S(1)} %copy-done, bf16[256,256]{1,0:T(8,128)(2,1)S(1)} %copy-done.1), custom_call_target="tpu_custom_call" | custom-call | tf_op jit(solution)/shard_map/pallas_call | solution.py:280
  5.6 0.0 copy-done.5
  6.3 0.0 copy-done.2
  6.3 0.0 copy-done.4
  6.3 15.3 %shard_map.83 = bf16[3,8,1280]{2,1,0:T(8,128)(2,1)S(1)} custom-call(s32[1]{0:T(128)S(6)} %copy.15.length_ref, s32[1,640]{1,0:T(1,128)S(1)} %broadcast_in_dim.6.pairs_ref, bf16[8,16,160]{2,1,0:T(8,128)(2,1)S(1)} %shard_map.82.send_ref, bf16[48,64]{1,0:T(8,128)(2,1)S(1)} %copy-done.4, s32[8,1280]{1,0:T(8,128)S(1)} %bitcast.11, bf16[4,8,1280]{2,1,0:T(8,128)(2,1)S(1)} %bitcast.12), custom_call_target="tpu_custom_call" | custom-call | tf_op jit(solution)/shard_map/pallas_call | solution.py:295
  21.7 0.6 %copy.16 = bf16[3,1,8,1,1280]{4,2,3,1,0:T(8,128)(2,1)} copy(bf16[3,1,8,1,1280]{4,2,3,1,0:T(8,128)(2,1)S(1)} %bitcast.10) | data formatting | bytes 122880
  (2 shorter events, 0.0 us)
Async XLA Ops:
  0.0 2.3 %copy-start = (bf16[80,8,1281]{2,1,0:T(8,128)(2,1)S(1)}, bf16[80,8,1281]{2,1,0:T(8,128)(2,1)}, u32[]{:S(2)}) copy-start(bf16[80,8,1281]{2,1,0:T(8,128)(2,1)} %legendre_ref.1) | copy-start | bytes 4919044
  0.0 2.3 %copy-start.1 = (bf16[256,256]{1,0:T(8,128)(2,1)S(1)}, bf16[256,256]{1,0:T(8,128)(2,1)}, u32[]{:S(2)}) copy-start(bf16[256,256]{1,0:T(8,128)(2,1)} %constant.2.clone.spread_ref) | copy-start | bytes 393220
  0.0 2.3 %copy-start.3 = (s32[640]{0:T(1024)S(1)}, s32[640]{0:T(1024)}, u32[]{:S(2)}) copy-start(s32[640]{0:T(1024)} %pairs_ref.1) | copy-start | bytes 7684
  2.2 3.4 %copy-start.5 = (s32[1,8,1,1280]{3,2,1,0:T(1,128)S(1)}, s32[1,8,1,1280]{3,2,1,0:T(1,128)}, u32[]{:S(2)}) copy-start(s32[1,8,1,1280]{3,2,1,0:T(1,128)} %param.12) | copy-start | bytes 122884
  2.2 4.1 %copy-start.2 = (bf16[4,1,8,1,1280]{4,2,3,1,0:T(8,128)(2,1)S(1)}, bf16[4,1,8,1,1280]{4,2,3,1,0:T(8,128)(2,1)}, u32[]{:S(2)}) copy-start(bf16[4,1,8,1,1280]{4,2,3,1,0:T(8,128)(2,1)} %param.13) | copy-start | bytes 245764
  2.2 4.1 %copy-start.4 = (bf16[48,64]{1,0:T(8,128)(2,1)S(1)}, bf16[48,64]{1,0:T(8,128)(2,1)}, u32[]{:S(2)}) copy-start(bf16[48,64]{1,0:T(8,128)(2,1)} %constant.6.clone.order_ref) | copy-start | bytes 18436

commit v5 on v3

--- a/solution.py
+++ b/solution.py
@@ -141,7 +141,8 @@
 
 
 def row_kernel(
-    seg_count, length_ref, pairs_ref, send_ref, order_ref, departure_ref, weights_ref, out_ref,
+    seg_count, length_ref, own_ref, pairs_ref, spectra_ref, legendre_ref, spread_ref, order_ref,
+    departure_ref, weights_ref, out_ref, rhs_ref, send_f, send_ref,
     table_ref, start_cos, start_sin, lhs_ref, grid_ref, recv_ref, fourier_ref, send_sem, recv_sem,
 ):
     length = length_ref[0]
@@ -149,12 +150,15 @@
     blocks = width // LANES
     greet, start, finish = exchange(send_ref, recv_ref, send_sem, recv_sem)
     greet()
+    pair_dev = legendre_ref.shape[0]
+    legendre_sums(
+        pair_dev, own_ref, spectra_ref, legendre_ref, spread_ref, send_ref, rhs_ref, send_f
+    )
     start()
     make_tables(seg_count, pairs_ref, length, table_ref, start_cos, start_sin)
     finish()
     along = lax.axis_size("lon")
     waves = lax.axis_size("wave")
-    pair_dev = pairs_ref.shape[1] // waves
     for i in range(waves):
         parts = jnp.concatenate([recv_ref[i * along + g] for g in range(along)], axis=0)
         ordered = jnp.dot(order_ref[...], parts, preferred_element_type=jnp.float32)
@@ -167,7 +171,7 @@
     depart(length // seg_count, blocks, levels, departure_ref, weights_ref, grid_ref, out_ref)
 
 
-def legendre_kernel(
+def legendre_sums(
     pair_dev, pairs_ref, spectra_ref, legendre_ref, spread_ref, send_ref, rhs_ref, send_f
 ):
     columns, padded, packed = spectra_ref.shape
@@ -247,26 +251,18 @@
     vmem = pl.BlockSpec(memory_space=pltpu.VMEM)
     smem = pl.BlockSpec(memory_space=pltpu.SMEM)
     wide = 2 * GROUP * row_total
-    send = pl.pallas_call(
-        functools.partial(legendre_kernel, pair_dev),
-        out_shape=jax.ShapeDtypeStruct((row_total, chunk, 2 * pair_dev), jnp.bfloat16),
-        in_specs=[smem] + [vmem] * 3,
-        out_specs=vmem,
-        scratch_shapes=[
-            pltpu.VMEM((padded // GROUP, wide, packed), jnp.bfloat16),
-            pltpu.VMEM((row_total, chunk, 2 * pair_dev), jnp.float32),
-        ],
-        compiler_params=pltpu.CompilerParams(vmem_limit_bytes=40 * 1024 * 1024),
-    )(pair_waves, flat_spec, legendre, lane_order(row_total))
     devices = lax.axis_size("wave") * seg_count
     blocks = width // LANES
     modes = 2 * pairs
     result = pl.pallas_call(
         functools.partial(row_kernel, seg_count),
         out_shape=jax.ShapeDtypeStruct((3, levels, width), jnp.bfloat16),
-        in_specs=[smem] + [vmem] * 5,
+        in_specs=[smem] * 2 + [vmem] * 7,
         out_specs=vmem,
         scratch_shapes=[
+            pltpu.VMEM((padded // GROUP, wide, packed), jnp.bfloat16),
+            pltpu.VMEM((row_total, chunk, 2 * pair_dev), jnp.float32),
+            pltpu.VMEM((row_total, chunk, 2 * pair_dev), jnp.bfloat16),
             pltpu.VMEM((SPAN, 2 * modes), jnp.bfloat16),
             pltpu.VMEM((16, modes), jnp.float32),
             pltpu.VMEM((16, modes), jnp.float32),
@@ -282,8 +278,11 @@
         ),
     )(
         row_lengths,
+        pair_waves,
         pair_waves[None, :],
-        send,
+        flat_spec,
+        legendre,
+        lane_order(row_total),
         row_order(levels, level_dev, chunk),
         departure[0, :, 0, :],
         weights[:, 0, :, 0, :],

time: 21.5 us -> 21.4 us (level)
  local copies, waits for them, and re-layouts: 2.92 us -> 4.39 us
  Pallas kernels: 17.5 us -> 16.2 us
    pallas_call x1 -> x0, Pallas kernels: 3.32 us -> none  [local(): pl.pallas_call(functools.partial(legendre_kernel, pair_dev), out_shape=ja...]
    pallas_call x1, Pallas kernels: 14.2 us -> 16.2 us  [local(): pl.pallas_call(functools.partial(row_kernel, seg_count), out_shape=jax.Sh...]
    unnamed x14 -> x12, local copies, waits for them, and re-layouts: 0.7 us -> 1.48 us
    broadcast_in_dim x1, local copies, waits for them, and re-layouts: 0.01 us -> 0.69 us  [local(): pair_waves[None, :]]
where the time goes in v5:
time: 21.4 us; the launch traced here: 21.2 us
  Pallas kernels  16.2 us (76%)
  local copies, waits for them, and re-layouts  4.39 us (21%)
  between operations  0.69 us (3%)
    pallas_call x1, Pallas kernels, local(): pl.pallas_call(functools.partial(row_kernel, seg_count), out_shape=jax.Sh...  16.2 us
    transpose x1, local copies, waits for them, and re-layouts, local(): jnp.transpose(spectra, (1, 2, 3, 0, 4)).reshape(columns, pair_dev, packed)  2.22 us
    unnamed x12, local copies, waits for them, and re-layouts  1.48 us
    broadcast_in_dim x1, local copies, waits for them, and re-layouts, local(): pair_waves[None, :]  0.69 us

profile of v5, /device:TPU:0, one launch (start us, length us, event | category | flops | bytes accessed | tf_op | source)
XLA Modules:
  0.0 21.2 jit_solution(1378303812660670900)
XLA Ops:
  0.7 0.7 %broadcast_in_dim.6.pairs_ref = s32[1,640]{1,0:T(1,128)S(1)} reshape(s32[640]{0:T(1024)} %own_ref.1) | data formatting | bytes 5120 | tf_op jit(solution)/shard_map/broadcast_in_dim | solution.py:282
  1.3 0.8 %copy.13 = s32[1,8,1,1280]{3,1,2,0:T(8,128)S(1)} copy(s32[1,8,1,1280]{3,2,1,0:T(1,128)} %param.12) | data formatting | bytes 81920
  2.1 0.0 copy-start
  2.1 0.0 copy-start.1
  2.1 0.0 copy-start.2
  2.1 0.0 copy-start.3
  2.1 0.0 copy-start.4
  2.2 2.2 %copy.9 = bf16[2,3,2,80,1281]{4,3,2,1,0:T(8,128)(2,1)S(1)} copy(bf16[2,3,2,80,1281]{4,2,1,0,3:T(2,128)(2,1)} %bitcast.13) | data formatting | bytes 4919040 | tf_op jit(solution)/shard_map/transpose | solution.py:249
  4.4 0.0 copy-done
  4.4 0.0 copy-done.1
  4.4 0.0 copy-done.2
  4.4 0.0 copy-done.3
  4.4 0.0 copy-done.4
  4.4 16.2 %shard_map.82 = bf16[3,8,1280]{2,1,0:T(8,128)(2,1)S(1)} custom-call(s32[1]{0:T(128)S(6)} %copy.15.length_ref, s32[640]{0:T(1024)S(1)} %copy-done.3, s32[1,640]{1,0:T(1,128)S(1)} %broadcast_in_dim.6.pairs_ref, bf16[12,80,1281]{2,1,0:T(8,128)(2,1)S(1)} %bitcast.9, bf16[80,8,1281]{2,1,0:T(8,128)(2,1)S(1)} %copy-done, bf16[256,256]{1,0:T(8,128)(2,1)S(1)} %copy-done.1, ...), custom_call_target="tpu_custom_call" | custom-call | tf_op jit(solution)/shard_map/pallas_call | solution.py:257
  20.6 0.6 %copy.16 = bf16[3,1,8,1,1280]{4,2,3,1,0:T(8,128)(2,1)} copy(bf16[3,1,8,1,1280]{4,2,3,1,0:T(8,128)(2,1)S(1)} %bitcast.10) | data formatting | bytes 122880
Async XLA Ops:
  2.1 2.3 %copy-start = (bf16[80,8,1281]{2,1,0:T(8,128)(2,1)S(1)}, bf16[80,8,1281]{2,1,0:T(8,128)(2,1)}, u32[]{:S(2)}) copy-start(bf16[80,8,1281]{2,1,0:T(8,128)(2,1)} %legendre_ref.1) | copy-start | bytes 4919044
  2.1 2.3 %copy-start.1 = (bf16[256,256]{1,0:T(8,128)(2,1)S(1)}, bf16[256,256]{1,0:T(8,128)(2,1)}, u32[]{:S(2)}) copy-start(bf16[256,256]{1,0:T(8,128)(2,1)} %constant.2.clone.spread_ref) | copy-start | bytes 393220
  2.1 2.3 %copy-start.2 = (bf16[4,1,8,1,1280]{4,2,3,1,0:T(8,128)(2,1)S(1)}, bf16[4,1,8,1,1280]{4,2,3,1,0:T(8,128)(2,1)}, u32[]{:S(2)}) copy-start(bf16[4,1,8,1,1280]{4,2,3,1,0:T(8,128)(2,1)} %param.13) | copy-start | bytes 245764
  2.1 2.3 %copy-start.3 = (s32[640]{0:T(1024)S(1)}, s32[640]{0:T(1024)}, u32[]{:S(2)}) copy-start(s32[640]{0:T(1024)} %own_ref.1) | copy-start | bytes 7684
  2.1 2.3 %copy-start.4 = (bf16[48,64]{1,0:T(8,128)(2,1)S(1)}, bf16[48,64]{1,0:T(8,128)(2,1)}, u32[]{:S(2)}) copy-start(bf16[48,64]{1,0:T(8,128)(2,1)} %constant.6.clone.order_ref) | copy-start | bytes 18436

commit v6 on v5

--- a/solution.py
+++ b/solution.py
@@ -31,7 +31,7 @@
 
 
 def make_tables(seg_count, pairs_ref, length, table_ref, start_cos, start_sin):
-    first = pairs_ref[...].astype(jnp.float32)
+    first = pairs_ref[...].reshape(1, -1).astype(jnp.float32)
     waves = jnp.concatenate([first, TRUNC - first], axis=1)
     modes = waves.shape[1]
     length_f = length.astype(jnp.float32)
@@ -142,11 +142,11 @@
 
 def row_kernel(
     seg_count, length_ref, own_ref, pairs_ref, spectra_ref, legendre_ref, spread_ref, order_ref,
-    departure_ref, weights_ref, out_ref, rhs_ref, send_f, send_ref,
+    departure_ref, weights_ref, out_ref, rhs_ref, send_f, send_ref, cells_ref,
     table_ref, start_cos, start_sin, lhs_ref, grid_ref, recv_ref, fourier_ref, send_sem, recv_sem,
 ):
     length = length_ref[0]
-    levels, width = departure_ref.shape
+    levels, _, width = departure_ref.shape
     blocks = width // LANES
     greet, start, finish = exchange(send_ref, recv_ref, send_sem, recv_sem)
     greet()
@@ -156,6 +156,8 @@
     )
     start()
     make_tables(seg_count, pairs_ref, length, table_ref, start_cos, start_sin)
+    for v in range(levels):
+        cells_ref[v : v + 1] = departure_ref[v]
     finish()
     along = lax.axis_size("lon")
     waves = lax.axis_size("wave")
@@ -168,7 +170,7 @@
     real = fourier_ref[: 3 * levels]
     imag = fourier_ref[3 * levels :]
     synthesize(real, imag, blocks, table_ref, start_cos, start_sin, lhs_ref, grid_ref)
-    depart(length // seg_count, blocks, levels, departure_ref, weights_ref, grid_ref, out_ref)
+    depart(length // seg_count, blocks, levels, cells_ref, weights_ref, grid_ref, out_ref)
 
 
 def legendre_sums(
@@ -263,6 +265,7 @@
             pltpu.VMEM((padded // GROUP, wide, packed), jnp.bfloat16),
             pltpu.VMEM((row_total, chunk, 2 * pair_dev), jnp.float32),
             pltpu.VMEM((row_total, chunk, 2 * pair_dev), jnp.bfloat16),
+            pltpu.VMEM((levels, width), jnp.int32),
             pltpu.VMEM((SPAN, 2 * modes), jnp.bfloat16),
             pltpu.VMEM((16, modes), jnp.float32),
             pltpu.VMEM((16, modes), jnp.float32),
@@ -279,12 +282,12 @@
     )(
         row_lengths,
         pair_waves,
-        pair_waves[None, :],
+        pair_waves,
         flat_spec,
         legendre,
         lane_order(row_total),
         row_order(levels, level_dev, chunk),
-        departure[0, :, 0, :],
+        departure[0],
         weights[:, 0, :, 0, :],
     )
     return result[:, None, :, None, :]

time: 21.4 us -> 19.9 us (0.930)
  local copies, waits for them, and re-layouts: 4.39 us -> 2.89 us
    unnamed x12 -> x13, local copies, waits for them, and re-layouts: 1.48 us -> 0.68 us
    broadcast_in_dim x1 -> x0, local copies, waits for them, and re-layouts: 0.69 us -> none  [local(): pair_waves[None, :]]
where the time goes in v6:
time: 19.9 us; the launch traced here: 19.8 us
  Pallas kernels  16.2 us (81%)
  local copies, waits for them, and re-layouts  2.89 us (15%)
  between operations  0.74 us (4%)
    pallas_call x1, Pallas kernels, local(): pl.pallas_call(functools.partial(row_kernel, seg_count), out_shape=jax.Sh...  16.2 us
    transpose x1, local copies, waits for them, and re-layouts, local(): jnp.transpose(spectra, (1, 2, 3, 0, 4)).reshape(columns, pair_dev, packed)  2.21 us
    unnamed x13, local copies, waits for them, and re-layouts  0.68 us

profile of v6, /device:TPU:0, one launch (start us, length us, event | category | flops | bytes accessed | tf_op | source)
XLA Modules:
  0.0 19.8 jit_solution(9631524673820143355)
XLA Ops:
  0.7 0.0 copy-start
  0.7 0.0 copy-start.1
  0.7 0.0 copy-start.2
  0.7 0.0 copy-start.3
  0.7 0.0 copy-start.4
  0.7 0.0 copy-start.5
  0.7 2.2 %copy.9 = bf16[2,3,2,80,1281]{4,3,2,1,0:T(8,128)(2,1)S(1)} copy(bf16[2,3,2,80,1281]{4,2,1,0,3:T(2,128)(2,1)} %bitcast.11) | data formatting | bytes 4919040 | tf_op jit(solution)/shard_map/transpose | solution.py:251
  2.9 0.0 copy-done
  3.0 0.0 copy-done.1
  3.0 0.0 copy-done.2
  3.0 0.0 copy-done.3
  3.0 0.0 copy-done.4
  3.0 0.0 copy-done.5
  3.0 16.2 %shard_map.82 = bf16[3,8,1280]{2,1,0:T(8,128)(2,1)S(1)} custom-call(s32[1]{0:T(128)S(6)} %copy.12.length_ref, s32[640]{0:T(1024)S(1)} %copy-done.4, s32[640]{0:T(1024)S(1)} %copy-done.4, bf16[12,80,1281]{2,1,0:T(8,128)(2,1)S(1)} %bitcast.7, bf16[80,8,1281]{2,1,0:T(8,128)(2,1)S(1)} %copy-done, bf16[256,256]{1,0:T(8,128)(2,1)S(1)} %copy-done.1, ...), custom_call_target="tpu_custom_call" | custom-call | tf_op jit(solution)/shard_map/pallas_call | solution.py:259
  19.2 0.6 %copy.13 = bf16[3,1,8,1,1280]{4,2,3,1,0:T(8,128)(2,1)} copy(bf16[3,1,8,1,1280]{4,2,3,1,0:T(8,128)(2,1)S(1)} %bitcast.8) | data formatting | bytes 122880
Async XLA Ops:
  0.7 2.3 %copy-start = (bf16[80,8,1281]{2,1,0:T(8,128)(2,1)S(1)}, bf16[80,8,1281]{2,1,0:T(8,128)(2,1)}, u32[]{:S(2)}) copy-start(bf16[80,8,1281]{2,1,0:T(8,128)(2,1)} %legendre_ref.1) | copy-start | bytes 4919044
  0.7 2.3 %copy-start.1 = (bf16[256,256]{1,0:T(8,128)(2,1)S(1)}, bf16[256,256]{1,0:T(8,128)(2,1)}, u32[]{:S(2)}) copy-start(bf16[256,256]{1,0:T(8,128)(2,1)} %constant.2.clone.spread_ref) | copy-start | bytes 393220
  0.7 2.3 %copy-start.2 = (bf16[4,1,8,1,1280]{4,2,3,1,0:T(8,128)(2,1)S(1)}, bf16[4,1,8,1,1280]{4,2,3,1,0:T(8,128)(2,1)}, u32[]{:S(2)}) copy-start(bf16[4,1,8,1,1280]{4,2,3,1,0:T(8,128)(2,1)} %param.13) | copy-start | bytes 245764
  0.7 2.3 %copy-start.3 = (s32[1,8,1,1280]{3,2,1,0:T(1,128)S(1)}, s32[1,8,1,1280]{3,2,1,0:T(1,128)}, u32[]{:S(2)}) copy-start(s32[1,8,1,1280]{3,2,1,0:T(1,128)} %param.12) | copy-start | bytes 122884
  0.7 2.3 %copy-start.4 = (s32[640]{0:T(1024)S(1)}, s32[640]{0:T(1024)}, u32[]{:S(2)}) copy-start(s32[640]{0:T(1024)} %pairs_ref.1) | copy-start | bytes 7684
  0.7 2.3 %copy-start.5 = (bf16[48,64]{1,0:T(8,128)(2,1)S(1)}, bf16[48,64]{1,0:T(8,128)(2,1)}, u32[]{:S(2)}) copy-start(bf16[48,64]{1,0:T(8,128)(2,1)} %constant.6.clone.order_ref) | copy-start | bytes 18436
